TPU v7x, 32 devices: a whole 2x2x4 slice. The times are simulated.
32 devices in a mesh: tensor: 2 (over x), serve: 16 (over z, y, core).
Axes of the slice: x: 2, y: 2, z: 4, core: 2. Of those that a mesh axis runs over, the one named last changes fastest.
Arguments:
- prefill: bfloat16 [32, 1024, 8192], P('serve', None, 'tensor'), may hold values from -6 to 6
- down_proj: bfloat16 [8192, 1024], P('tensor'), may hold values from -0.0625 to 0.0625
- up_key: bfloat16 [512, 1024], P(None, 'tensor'), may hold values from -0.25 to 0.25
- up_value: bfloat16 [512, 1024], P(None, 'tensor'), may hold values from -0.25 to 0.25
- queries: bfloat16 [32, 4, 8192], P('serve', None, 'tensor'), may hold values from -60 to 60
- cache_latent: bfloat16 [32, 1024, 1024], P('serve'), may hold values from -60 to 60
- hist_len: int32 [32], P('serve'), may hold values from 256 to 1024, as said below
- assign: int32 [32], replicated, may hold values from 0 to 31, each once
Outputs:
- attn: bfloat16 [32, 4, 8192], P('serve', None, 'tensor')
- span_latent: bfloat16 [32, 1024, 1024], P('serve', None, 'tensor')
Inputs may be any that keep to these rules, and one draw needn't show every extreme that they name: `hist_len`: some slot has exactly 1024 live rows. `assign`: each slot receives exactly one request's span.
All inputs are finite; a program needn't handle non-finite values.
Results may differ from a plain program's by a relative error of at most 0.012.
The roundings to bfloat16 on the way count: a program that leaves them out, or rounds other values in their place, can miss the bound.
Values may be sent and summed in bfloat16 or wider, within the bound.
A program may use at most 128 MiB of HBM per device.

v0:
```python
import jax
import jax.numpy as jnp
from jax import lax
from jax.sharding import PartitionSpec as P

HEAD_DIM = 128


ROPE_BASE = 500000.0


def rotate(vectors, positions):
    half = vectors.shape[-1] // 2
    frequency = ROPE_BASE ** (-jnp.arange(half, dtype=jnp.float32) / half)
    angles = positions.astype(jnp.float32)[..., None, None] * frequency
    cosine = jnp.cos(angles)
    sine = jnp.sin(angles)
    first_half = vectors[..., :half]
    second_half = vectors[..., half:]
    return jnp.concatenate(
        [first_half * cosine - second_half * sine, second_half * cosine + first_half * sine],
        axis=-1,
    )


def project_rows(prefill, down_proj):
    return lax.psum_scatter(
        jnp.einsum("ctd,dr->tcr", prefill, down_proj, preferred_element_type=jnp.float32),
        "tensor",
        scatter_dimension=0,
        tiled=True,
    )


def shards(prefill, down_proj, up_key, up_value, queries, cache_latent, hist_len, assign):
    slot_count, span_count, feature_count = prefill.shape
    tensor_count = lax.axis_size("tensor")
    serve_count = lax.axis_size("serve")
    latent_width = down_proj.shape[1]
    rank_width = latent_width // 2
    column_count = latent_width // tensor_count
    request_count = assign.shape[0]
    source_of = (
        jnp.zeros((request_count,), jnp.int32)
        .at[assign]
        .set(jnp.arange(request_count, dtype=jnp.int32))
    )
    finished = project_rows(prefill, down_proj).astype(jnp.bfloat16)
    piece_rows = finished.shape[0] // serve_count
    spread = lax.all_to_all(
        finished.reshape(serve_count, piece_rows, slot_count, latent_width),
        "serve",
        split_axis=0,
        concat_axis=2,
        tiled=True,
    )
    by_slot = jnp.swapaxes(spread.reshape(piece_rows, request_count, latent_width), 0, 1)[source_of]
    arrived = lax.all_to_all(by_slot, "serve", split_axis=0, concat_axis=1, tiled=True)
    joined = lax.all_gather(arrived, "tensor", axis=1, tiled=True)
    span_out = lax.dynamic_slice_in_dim(
        joined, lax.axis_index("tensor") * column_count, column_count, 2
    )
    kv_local = up_key.shape[1] // HEAD_DIM
    head_local = queries.shape[2] // HEAD_DIM
    group_size = head_local // kv_local
    history = cache_latent.shape[1]
    step_count = queries.shape[1]
    score_scale = HEAD_DIM ** (-0.5)
    cache_keys = jnp.dot(cache_latent[..., :rank_width], up_key, preferred_element_type=jnp.float32)
    cache_keys = cache_keys.reshape(slot_count, history, kv_local, HEAD_DIM)
    cache_pos = jnp.broadcast_to(
        jnp.arange(history, dtype=jnp.int32)[None, :], (slot_count, history)
    )
    cache_keys = rotate(cache_keys, cache_pos).astype(jnp.bfloat16)
    cache_values = jnp.dot(
        cache_latent[..., rank_width:], up_value, preferred_element_type=jnp.float32
    ).astype(jnp.bfloat16)
    cache_values = cache_values.reshape(slot_count, history, kv_local, HEAD_DIM)
    span_keys = jnp.dot(joined[..., :rank_width], up_key, preferred_element_type=jnp.float32)
    span_keys = span_keys.reshape(slot_count, span_count, kv_local, HEAD_DIM)
    span_pos = hist_len[:, None] + jnp.arange(span_count, dtype=jnp.int32)[None, :]
    span_keys = rotate(span_keys, span_pos).astype(jnp.bfloat16)
    span_values = jnp.dot(
        joined[..., rank_width:], up_value, preferred_element_type=jnp.float32
    ).astype(jnp.bfloat16)
    span_values = span_values.reshape(slot_count, span_count, kv_local, HEAD_DIM)
    query_pos = hist_len[:, None] + span_count + jnp.arange(step_count, dtype=jnp.int32)[None, :]
    rotated = rotate(
        queries.astype(jnp.float32).reshape(slot_count, step_count, head_local, HEAD_DIM), query_pos
    ).astype(jnp.bfloat16)
    rotated = rotated.reshape(slot_count, step_count, kv_local, group_size, HEAD_DIM)
    cache_scores = (
        jnp.einsum("cskgd,cnkd->cskgn", rotated, cache_keys, preferred_element_type=jnp.float32)
        * score_scale
    )
    live = jnp.arange(history, dtype=jnp.int32)[None, :] < hist_len[:, None]
    cache_scores = jnp.where(live[:, None, None, None, :], cache_scores, -jnp.inf)
    span_scores = (
        jnp.einsum("cskgd,cmkd->cskgm", rotated, span_keys, preferred_element_type=jnp.float32)
        * score_scale
    )
    highest = jnp.maximum(jnp.max(cache_scores, axis=-1), jnp.max(span_scores, axis=-1))
    cache_weights = jnp.exp(cache_scores - highest[..., None])
    span_weights = jnp.exp(span_scores - highest[..., None])
    totals = jnp.sum(cache_weights, axis=-1) + jnp.sum(span_weights, axis=-1)
    cache_probs = (cache_weights / totals[..., None]).astype(jnp.bfloat16)
    span_probs = (span_weights / totals[..., None]).astype(jnp.bfloat16)
    mixed = jnp.einsum(
        "cskgn,cnkd->cskgd", cache_probs, cache_values, preferred_element_type=jnp.float32
    )
    mixed = mixed + jnp.einsum(
        "cskgm,cmkd->cskgd", span_probs, span_values, preferred_element_type=jnp.float32
    )
    attn = mixed.astype(jnp.bfloat16).reshape(slot_count, step_count, head_local * HEAD_DIM)
    return (attn, span_out)


def solution(mesh):
    return jax.shard_map(
        shards,
        mesh=mesh,
        in_specs=(
            P("serve", None, "tensor"),
            P("tensor", None),
            P(None, "tensor"),
            P(None, "tensor"),
            P("serve", None, "tensor"),
            P("serve", None, None),
            P("serve"),
            P(),
        ),
        out_specs=(P("serve", None, "tensor"), P("serve", None, "tensor")),
        check_vma=False,
    )
```

profile of v0, /device:TPU:17, one launch (start us, length us, event | category | flops | bytes accessed | tf_op | source)
XLA Modules:
  0.0 344.3 jit_solution(15017379745211808564)
XLA Ops:
  7.2 0.0 copy-start
  7.2 0.0 reduce-scatter.2.cloned.1.call-start
  7.2 24.3 %fusion.2 = f32[1024,2,1024]{0,2,1:T(8,128)} fusion(bf16[2,1024,4096]{2,1,0:T(8,128)(2,1)} %param.8, bf16[4096,1024]{1,0:T(8,128)(2,1)} %param.9), kind=kOutput, calls=%fused_computation.8 | convolution fusion | flops 17179869184 | bytes 33554432 | tf_op jit(solution)/shard_map/ctd,dr->tcr/dot_general | solution.py:28
  31.5 0.0 reduce-scatter.2.cloned.1.call-update
  31.6 100.5 %reduce-scatter.2.cloned.1.call-done = f32[512,2,1024]{0,2,1:T(8,128)} async-done(((f32[1024,2,1024]{0,2,1:T(8,128)}), f32[512,2,1024]{0,2,1:T(8,128)}) %reduce-scatter.2.cloned.1.call-update) | async-done | bytes 4194320 | tf_op jit(solution)/shard_map/reduce_scatter | solution.py:27
  132.0 2.5 convert_element_type.53
  134.5 2.4 copy.45
  136.9 3.2 copy.46
  140.1 6.5 %all-to-all-start = ((bf16[16,32,2,1024]{3,1,2,0:T(8,128)(2,1)}), bf16[16,32,2,1024]{3,1,2,0:T(8,128)(2,1)S(1)}, u32[]{:S(2)}, u32[]{:S(2)}) async-start(bf16[16,32,2,1024]{3,1,2,0:T(8,128)(2,1)} %copy.46), calls=%async_computation.1 | async-start | bytes 4194304 | tf_op jit(solution)/shard_map/all_to_all | solution.py:50
  146.6 0.0 all-gather.2.cloned.1.call-start
  146.6 0.0 copy-done.6
  146.6 0.7 scatter_custom_fusion
  147.4 46.4 %all-to-all-done = bf16[16,32,2,1024]{3,1,2,0:T(8,128)(2,1)S(1)} async-done(((bf16[16,32,2,1024]{3,1,2,0:T(8,128)(2,1)}), bf16[16,32,2,1024]{3,1,2,0:T(8,128)(2,1)S(1)}, u32[]{:S(2)}, u32[]{:S(2)}) %all-to-all-start) | async-done | bytes 2097184 | tf_op jit(solution)/shard_map/all_to_all | solution.py:50
  193.7 2.0 gather_fusion
  195.7 52.1 %all_to_all.33 = bf16[32,32,1024]{2,1,0:T(8,128)(2,1)S(1)} all-to-all(bf16[32,32,1024]{2,1,0:T(8,128)(2,1)} %gather_fusion), channel_id=1, replica_groups=mesh['tensor'=2,'serve'=16] {'serve'}, dimensions={0} | all-to-all | bytes 4194304 | tf_op jit(solution)/shard_map/all_to_all | solution.py:58
  247.8 1.5 copy.47
  249.3 0.0 all-gather.2.cloned.1.call-update
  249.3 0.0 copy-done
  249.3 2.9 fusion.15
  252.2 1.8 fusion.50
  254.0 4.0 %copy.74 = f32[2,1024,4,64]{3,1,2,0:T(8,128)} copy(f32[2,1024,4,64]{1,3,2,0:T(8,128)} %get-tuple-element.11) | data formatting | bytes 4194304
  258.0 2.8 copy.75
  260.7 0.1 reshape.150
  260.9 0.1 add_convert_fusion.4
  260.9 0.1 iota_compare_fusion
  261.0 0.1 add_convert_fusion.3
  261.1 0.1 multiply_cosine_fusion.2
  261.2 0.1 fusion.41
  261.3 0.0 copy-start.2
  261.3 7.3 %multiply_cosine_fusion = (f32[2,1024,64]{2,1,0:T(8,128)}, f32[2,1024,64]{2,1,0:T(8,128)}, f32[2,1024,64]{2,1,0:T(8,128)}, f32[2,1024,64]{2,1,0:T(8,128)}) fusion(f32[2,1024]{1,0:T(2,128)S(1)} %add_convert_fusion.3, f32[64]{0:T(128)S(1)} %multiply_power_fusion, f32[1024]{0:T(1024)S(1)} %iota_convert_fusion), kind=kLoop, calls=%fused_computation.28 | loop fusion | flops 262144 | bytes 2109696 | tf_op jit(solution)/shard_map/cos | solution.py:16
  268.6 0.0 copy-done.5
  268.6 2.6 fusion.19
  271.2 34.1 %all-gather.2.cloned.1.call-done = bf16[2,1024,1024]{2,1,0:T(8,128)(2,1)} async-done(((bf16[2,512,1024]{2,1,0:T(8,128)(2,1)}), bf16[2,1024,1024]{2,1,0:T(8,128)(2,1)}) %all-gather.2.cloned.1.call-update) | async-done | bytes 4194320 | tf_op jit(solution)/shard_map/all_gather | solution.py:59
  305.4 2.9 fusion.7
  308.3 1.8 fusion.49
  310.1 3.8 %copy.76 = f32[2,1024,4,64]{3,1,2,0:T(8,128)} copy(f32[2,1024,4,64]{1,3,2,0:T(8,128)} %get-tuple-element.9) | data formatting | bytes 4194304
  313.8 2.7 copy.77
  316.5 8.4 %subtract_convert_fusion = (bf16[2,1024,4,64]{3,1,2,0:T(8,128)(2,1)S(1)}, bf16[2,1024,4,64]{3,1,2,0:T(8,128)(2,1)S(1)}, bf16[2,1024,4,64]{3,1,2,0:T(8,128)(2,1)S(1)}, bf16[2,1024,4,64]{3,1,2,0:T(8,128)(2,1)S(1)}) fusion(f32[2,1024,4,64]{3,1,2,0:T(8,128)} %copy.77, f32[2,1024,4,64]{3,1,2,0:T(8,128)} %copy.76, f32[2,1024,64]{2,1,0:T(8,128)} %get-tuple-element.15, ...), kind=kLoop, calls=%fused_computation.5 | loop fusion | flops 8388608 | bytes 14680064 | tf_op jit(solution)/shard_map/convert.1
  324.9 1.4 fusion.52
  326.3 1.4 fusion.51
  327.7 0.5 fusion.33
  328.2 1.1 copy-done.7
  329.3 0.8 fusion.40
  330.2 1.4 copy-done.1
  331.5 1.3 fusion.22
  332.8 0.8 fusion.31
  333.7 0.7 reshape.148
  334.4 3.0 constant_dynamic-slice_fusion
  (19 shorter events, 0.1 us)
Async XLA Ops:
  7.2 242.1 %copy-start = (bf16[512,512]{1,0:T(8,128)(2,1)S(1)}, bf16[512,512]{1,0:T(8,128)(2,1)}, u32[]{:S(2)}) copy-start(bf16[512,512]{1,0:T(8,128)(2,1)} %param.10) | copy-start | bytes 1572868
  7.2 124.9 %reduce-scatter.2.cloned.1.call-start = ((), (), s32[]{:S(2)}) async-start(), calls=%async_computation.3 | async-start | bytes 12582912 | tf_op jit(solution)/shard_map/reduce_scatter | solution.py:27
  140.1 6.5 %copy-start.6 = (s32[32]{0:T(128)S(1)}, s32[32]{0:T(128)}, u32[]{:S(2)}) copy-start(s32[32]{0:T(128)} %param.15) | copy-start | bytes 388
  140.1 53.6 %all-to-all-start = ((bf16[16,32,2,1024]{3,1,2,0:T(8,128)(2,1)}), bf16[16,32,2,1024]{3,1,2,0:T(8,128)(2,1)S(1)}, u32[]{:S(2)}, u32[]{:S(2)}) async-start(bf16[16,32,2,1024]{3,1,2,0:T(8,128)(2,1)} %copy.46), calls=%async_computation.1 | async-start | bytes 4194304 | tf_op jit(solution)/shard_map/all_to_all | solution.py:50
  146.6 158.8 %all-gather.2.cloned.1.call-start = ((), (), s32[]{:S(2)}) async-start(), calls=%async_computation.4 | async-start | bytes 6291456 | tf_op jit(solution)/shard_map/all_gather | solution.py:59
  257.9 2.8 copy-start.3
  258.0 2.9 copy-start.4
  258.0 10.6 %copy-start.5 = (bf16[512,512]{1,0:T(8,128)(2,1)S(1)}, bf16[512,512]{1,0:T(8,128)(2,1)}, u32[]{:S(2)}) copy-start(bf16[512,512]{1,0:T(8,128)(2,1)} %param.11) | copy-start | bytes 1572868
  261.3 7.3 %copy-start.2 = (bf16[2,1024,1024]{2,1,0:T(8,128)(2,1)S(1)}, bf16[2,1024,1024]{2,1,0:T(8,128)(2,1)}, u32[]{:S(2)}) copy-start(bf16[2,1024,1024]{2,1,0:T(8,128)(2,1)} %param.13) | copy-start | bytes 12582916
  327.7 1.6 copy-start.7
  329.3 2.2 copy-start.1
Sparse Core Ops, SparseCore 0:
  31.7 100.2 reduce-scatter.1
  249.4 55.9 all-gather.1
where the time goes:
time: 346 us; the launch traced here: 344 us
  waiting for transfers between devices  181 us (52%)
  blocking collectives  52.1 us (15%)
  matrix products  38.6 us (11%)
  local copies, waits for them, and re-layouts  32.8 us (9%)
  other arithmetic  19 us (5%)
  between operations  14.2 us (4%)
  starting transfers between devices  6.56 us (2%)
    reduce_scatter x1, waiting for transfers between devices, project_rows(): lax.psum_scatter(jnp.einsum('ctd,dr->tcr', prefill, down_proj, preferred_...  100 us
    all_to_all x1, blocking collectives, shards(): lax.all_to_all(by_slot, 'serve', split_axis=0, concat_axis=1, tiled=True)  52.1 us
    all_to_all x1, waiting for transfers between devices, shards(): lax.all_to_all(finished.reshape(serve_count, piece_rows, slot_count, late...  46.4 us
    all_gather x1, waiting for transfers between devices, shards(): joined = lax.all_gather(arrived, 'tensor', axis=1, tiled=True)  34.1 us
    dot_general x1, matrix products, project_rows(): jnp.einsum('ctd,dr->tcr', prefill, down_proj, preferred_element_type=jnp....  24.3 us
    unnamed x20, local copies, waits for them, and re-layouts  15.7 us
    another operation x1, other arithmetic  8.35 us
    cos x2, other arithmetic, rotate(): cosine = jnp.cos(angles)  7.38 us
  transfers between devices with their start and end apart: 3, of which 3 were waited for; matrix products, arithmetic and copies ran while one was open for 7% of the time, Pallas kernels for 0%

commit v1 on v0

--- a/solution.py
+++ b/solution.py
@@ -1,6 +1,10 @@
+import functools
+
 import jax
 import jax.numpy as jnp
 from jax import lax
+from jax.experimental import pallas as pl
+from jax.experimental.pallas import tpu as pltpu
 from jax.sharding import PartitionSpec as P
 
 HEAD_DIM = 128
@@ -23,43 +27,258 @@
     )
 
 
-def project_rows(prefill, down_proj):
-    return lax.psum_scatter(
-        jnp.einsum("ctd,dr->tcr", prefill, down_proj, preferred_element_type=jnp.float32),
-        "tensor",
-        scatter_dimension=0,
-        tiled=True,
-    )
+MESH = pl.DeviceIdType.MESH
+LAG = 2
+
+
+def hand_off_kernel(
+    prefill_ref,
+    down_ref,
+    source_ref,
+    mine_out,
+    other_out,
+    tokens,
+    partial,
+    arrived_partial,
+    own,
+    piece,
+    spread,
+    staged,
+    mine,
+    other,
+    load_sem,
+    partial_send,
+    partial_recv,
+    spread_send,
+    spread_recv,
+    home_send,
+    home_recv,
+    share_send,
+    share_recv,
+    store_sem,
+):
+    serve_count, slot_count, rows, width = piece.shape
+    tensor = lax.axis_index("tensor")
+    serve = lax.axis_index("serve")
+    peer = 1 - tensor
+
+    barrier = pltpu.get_barrier_semaphore()
+    pl.semaphore_signal(barrier, inc=1, device_id={"tensor": peer}, device_id_type=MESH)
+
+    @pl.loop(1, serve_count)
+    def _(step):
+        pl.semaphore_signal(
+            barrier,
+            inc=1,
+            device_id={"serve": lax.rem(serve + step, serve_count)},
+            device_id_type=MESH,
+        )
+
+    def target(step):
+        return lax.rem(serve + step + 1, serve_count)
+
+    def origin(step):
+        return lax.rem(serve + 2 * serve_count - step - 1, serve_count)
+
+    def load(step):
+        start = pl.multiple_of(target(step) * rows, rows)
+        return pltpu.make_async_copy(
+            prefill_ref.at[:, pl.ds(start, rows), :],
+            tokens.at[lax.rem(step, 2)],
+            load_sem.at[lax.rem(step, 2)],
+        )
+
+    def partial_copy(step):
+        return pltpu.make_async_remote_copy(
+            src_ref=partial.at[step],
+            dst_ref=arrived_partial.at[step],
+            send_sem=partial_send.at[step],
+            recv_sem=partial_recv.at[step],
+            device_id={"tensor": peer},
+            device_id_type=MESH,
+        )
+
+    def spread_copy(step, place):
+        return pltpu.make_async_remote_copy(
+            src_ref=piece.at[step],
+            dst_ref=spread.at[place],
+            send_sem=spread_send.at[step],
+            recv_sem=spread_recv.at[place],
+            device_id={"serve": target(step)},
+            device_id_type=MESH,
+        )
+
+    def home_copy(step, place):
+        start = pl.multiple_of(place * rows, rows)
+        return pltpu.make_async_remote_copy(
+            src_ref=staged.at[step],
+            dst_ref=mine.at[:, pl.ds(start, rows), :],
+            send_sem=home_send.at[step],
+            recv_sem=home_recv.at[place],
+            device_id={"serve": target(step)},
+            device_id_type=MESH,
+        )
+
+    def share_copy(place):
+        start = pl.multiple_of(place * rows, rows)
+        return pltpu.make_async_remote_copy(
+            src_ref=mine.at[:, pl.ds(start, rows), :],
+            dst_ref=other.at[:, pl.ds(start, rows), :],
+            send_sem=share_send.at[place],
+            recv_sem=share_recv.at[place],
+            device_id={"tensor": peer},
+            device_id_type=MESH,
+        )
+
+    load(0).start()
+    pl.semaphore_wait(barrier, serve_count)
+    peer_columns = pl.ds(pl.multiple_of(peer * width, width), width)
+    own_columns = pl.ds(pl.multiple_of(tensor * width, width), width)
+
+    def project(step):
+        load(step).wait()
+
+        @pl.when(step + 1 < serve_count)
+        def _():
+            load(step + 1).start()
+
+        block = tokens[lax.rem(step, 2)].reshape(slot_count * rows, -1)
+        partial[step] = jnp.dot(
+            block, down_ref[:, peer_columns], preferred_element_type=jnp.float32
+        ).astype(jnp.bfloat16)
+        partial_copy(step).start()
+        own[step] = jnp.dot(block, down_ref[:, own_columns], preferred_element_type=jnp.float32)
+
+    def finish(step):
+        partial_copy(step).wait_recv()
+        latent = (own[step] + arrived_partial[step].astype(jnp.float32)).astype(jnp.bfloat16)
+        latent = latent.reshape(slot_count, rows, width)
+
+        @pl.when(step < serve_count - 1)
+        def _():
+            piece[step] = latent
+            spread_copy(step, serve).start()
+
+        @pl.when(step == serve_count - 1)
+        def _():
+            spread[serve] = latent
+
+    @pl.loop(0, serve_count)
+    def _(step):
+        project(step)
+
+        @pl.when(step >= LAG)
+        def _():
+            finish(step - LAG)
+
+    @pl.loop(serve_count - LAG, serve_count)
+    def _(step):
+        finish(step)
+
+    @pl.loop(0, serve_count - 1)
+    def _(step):
+        spread_copy(step, origin(step)).wait_recv()
+
+    @pl.loop(0, serve_count)
+    def _(step):
+        for index in range(slot_count):
+            source = source_ref[target(step) * slot_count + index]
+            staged[step, index] = spread[source // slot_count, lax.rem(source, slot_count)]
+
+        @pl.when(step < serve_count - 1)
+        def _():
+            home_copy(step, serve).start()
+
+        @pl.when(step == serve_count - 1)
+        def _():
+            start = pl.multiple_of(serve * rows, rows)
+            mine[:, pl.ds(start, rows), :] = staged[step]
+            share_copy(serve).start()
+
+    @pl.loop(0, serve_count - 1)
+    def _(step):
+        place = origin(step)
+        home_copy(step, place).wait_recv()
+        share_copy(place).start()
+
+    mine_store = pltpu.make_async_copy(mine, mine_out, store_sem.at[0])
+    mine_store.start()
+
+    @pl.loop(0, serve_count)
+    def _(step):
+        share_copy(step).wait()
+        partial_copy(step).wait_send()
+
+        @pl.when(step < serve_count - 1)
+        def _():
+            spread_copy(step, serve).wait_send()
+            home_copy(step, serve).wait_send()
+
+    other_store = pltpu.make_async_copy(other, other_out, store_sem.at[1])
+    other_store.start()
+    other_store.wait()
+    mine_store.wait()
+
+
+def hand_off(prefill, down_proj, source_of):
+    slot_count, span_count, feature_count = prefill.shape
+    serve_count = lax.axis_size("serve")
+    width = down_proj.shape[1] // lax.axis_size("tensor")
+    rows = span_count // serve_count
+    half = jax.ShapeDtypeStruct((slot_count, span_count, width), jnp.bfloat16)
+    pieces = (serve_count, slot_count, rows, width)
+    flat = (serve_count, slot_count * rows, width)
+    each = pltpu.SemaphoreType.DMA((serve_count,))
+    return pl.pallas_call(
+        hand_off_kernel,
+        out_shape=(half, half),
+        in_specs=[
+            pl.BlockSpec(memory_space=pl.ANY),
+            pl.BlockSpec(memory_space=pltpu.VMEM),
+            pl.BlockSpec(memory_space=pltpu.SMEM),
+        ],
+        out_specs=(pl.BlockSpec(memory_space=pl.ANY), pl.BlockSpec(memory_space=pl.ANY)),
+        scratch_shapes=[
+            pltpu.VMEM((2, slot_count, rows, feature_count), jnp.bfloat16),
+            pltpu.VMEM(flat, jnp.bfloat16),
+            pltpu.VMEM(flat, jnp.bfloat16),
+            pltpu.VMEM(flat, jnp.float32),
+            pltpu.VMEM(pieces, jnp.bfloat16),
+            pltpu.VMEM(pieces, jnp.bfloat16),
+            pltpu.VMEM(pieces, jnp.bfloat16),
+            pltpu.VMEM(half.shape, jnp.bfloat16),
+            pltpu.VMEM(half.shape, jnp.bfloat16),
+            pltpu.SemaphoreType.DMA((2,)),
+            each,
+            each,
+            each,
+            each,
+            each,
+            each,
+            each,
+            each,
+            pltpu.SemaphoreType.DMA((2,)),
+        ],
+        compiler_params=pltpu.CompilerParams(
+            collective_id=0, has_side_effects=True, vmem_limit_bytes=56 * 2**20
+        ),
+        cost_estimate=pl.CostEstimate(
+            flops=4 * slot_count * span_count * feature_count * width,
+            bytes_accessed=2 * slot_count * span_count * feature_count,
+            transcendentals=0,
+        ),
+    )(prefill, down_proj, source_of)
 
 
 def shards(prefill, down_proj, up_key, up_value, queries, cache_latent, hist_len, assign):
-    slot_count, span_count, feature_count = prefill.shape
-    tensor_count = lax.axis_size("tensor")
-    serve_count = lax.axis_size("serve")
-    latent_width = down_proj.shape[1]
-    rank_width = latent_width // 2
-    column_count = latent_width // tensor_count
-    request_count = assign.shape[0]
-    source_of = (
-        jnp.zeros((request_count,), jnp.int32)
-        .at[assign]
-        .set(jnp.arange(request_count, dtype=jnp.int32))
-    )
-    finished = project_rows(prefill, down_proj).astype(jnp.bfloat16)
-    piece_rows = finished.shape[0] // serve_count
-    spread = lax.all_to_all(
-        finished.reshape(serve_count, piece_rows, slot_count, latent_width),
-        "serve",
-        split_axis=0,
-        concat_axis=2,
-        tiled=True,
-    )
-    by_slot = jnp.swapaxes(spread.reshape(piece_rows, request_count, latent_width), 0, 1)[source_of]
-    arrived = lax.all_to_all(by_slot, "serve", split_axis=0, concat_axis=1, tiled=True)
-    joined = lax.all_gather(arrived, "tensor", axis=1, tiled=True)
-    span_out = lax.dynamic_slice_in_dim(
-        joined, lax.axis_index("tensor") * column_count, column_count, 2
-    )
+    slot_count, span_count, _ = prefill.shape
+    rank_width = down_proj.shape[1] // 2
+    request = jnp.arange(assign.shape[0], dtype=jnp.int32)
+    source_of = jnp.sum(jnp.where(assign[None, :] == request[:, None], request[None, :], 0), axis=1)
+    span_out, other = hand_off(prefill, down_proj, source_of)
+    first = lax.axis_index("tensor") == 0
+    key_latent = jnp.where(first, span_out, other)
+    value_latent = jnp.where(first, other, span_out)
     kv_local = up_key.shape[1] // HEAD_DIM
     head_local = queries.shape[2] // HEAD_DIM
     group_size = head_local // kv_local
@@ -76,12 +295,12 @@
         cache_latent[..., rank_width:], up_value, preferred_element_type=jnp.float32
     ).astype(jnp.bfloat16)
     cache_values = cache_values.reshape(slot_count, history, kv_local, HEAD_DIM)
-    span_keys = jnp.dot(joined[..., :rank_width], up_key, preferred_element_type=jnp.float32)
+    span_keys = jnp.dot(key_latent, up_key, preferred_element_type=jnp.float32)
     span_keys = span_keys.reshape(slot_count, span_count, kv_local, HEAD_DIM)
     span_pos = hist_len[:, None] + jnp.arange(span_count, dtype=jnp.int32)[None, :]
     span_keys = rotate(span_keys, span_pos).astype(jnp.bfloat16)
     span_values = jnp.dot(
-        joined[..., rank_width:], up_value, preferred_element_type=jnp.float32
+        value_latent, up_value, preferred_element_type=jnp.float32
     ).astype(jnp.bfloat16)
     span_values = span_values.reshape(slot_count, span_count, kv_local, HEAD_DIM)
     query_pos = hist_len[:, None] + span_count + jnp.arange(step_count, dtype=jnp.int32)[None, :]

time: 346 us -> 205 us (0.59)
  waiting for transfers between devices: 181 us -> 0 us
  Pallas kernels: 0 us -> 148 us
  blocking collectives: 52.1 us -> 0 us
  matrix products: 38.6 us -> 13.7 us
  between operations: 14.2 us -> 0.79 us
  local copies, waits for them, and re-layouts: 32.8 us -> 20.8 us
  starting transfers between devices: 6.56 us -> 0 us
    pallas_call x0 -> x1, Pallas kernels: none -> 148 us  [hand_off(): pl.pallas_call(hand_off_kernel, out_shape=(half, half), in_specs=[pl.Bloc...]
    reduce_scatter x1 -> x0, waiting for transfers between devices: 100 us -> none  [project_rows(): lax.psum_scatter(jnp.einsum('ctd,dr->tcr', prefill, down_proj, preferred_...]
    all_to_all x1 -> x0, blocking collectives: 52.1 us -> none  [shards(): lax.all_to_all(by_slot, 'serve', split_axis=0, concat_axis=1, tiled=True)]
    all_to_all x1 -> x0, waiting for transfers between devices: 46.4 us -> none  [shards(): lax.all_to_all(finished.reshape(serve_count, piece_rows, slot_count, late...]
    all_gather x1 -> x0, waiting for transfers between devices: 34.1 us -> none  [shards(): joined = lax.all_gather(arrived, 'tensor', axis=1, tiled=True)]
    dot_general x3 -> x2, matrix products: 28.5 us -> 4.2 us  [the longest x1 2.9 us: shards(): span_keys = jnp.dot(key_latent, up_key, preferred_element_type=jnp.float32)]
    all_to_all x1 -> x0, starting transfers between devices: 6.49 us -> none  [shards(): lax.all_to_all(finished.reshape(serve_count, piece_rows, slot_count, late...]
    unnamed x20 -> x25, local copies, waits for them, and re-layouts: 15.7 us -> 16.5 us
  transfers between devices with their start and end apart: 3 -> 0, of which waited for: 3 -> 0; matrix products, arithmetic and copies ran while one was open for 7% -> 0% of each run, Pallas kernels for 0% -> 0%
where the time goes in v1:
time: 205 us; the launch traced here: 204 us
  Pallas kernels  148 us (72%)
  local copies, waits for them, and re-layouts  20.8 us (10%)
  other arithmetic  20 us (10%)
  matrix products  13.7 us (7%)
    pallas_call x1, Pallas kernels, hand_off(): pl.pallas_call(hand_off_kernel, out_shape=(half, half), in_specs=[pl.Bloc...  148 us
    unnamed x25, local copies, waits for them, and re-layouts  16.5 us
    another operation x1, other arithmetic  10.6 us
    cos x2, other arithmetic, rotate(): cosine = jnp.cos(angles)  7.22 us

profile of v1, /device:TPU:17, one launch (start us, length us, event | category | flops | bytes accessed | tf_op | source)
XLA Modules:
  0.0 203.6 jit_solution(3967971978914073072)
XLA Ops:
  0.6 0.0 copy-start
  0.6 1.3 select_reduce_fusion.source_ref
  2.0 148.4 %shard_map.95 = (bf16[2,1024,512]{2,1,0:T(8,128)(2,1)}, bf16[2,1024,512]{2,1,0:T(8,128)(2,1)}) custom-call(bf16[2,1024,4096]{2,1,0:T(8,128)(2,1)} %prefill_ref.1, bf16[4096,1024]{1,0:T(8,128)(2,1)} %down_ref.1, s32[32]{0:T(128)} %select_reduce_fusion.source_ref), custom_call_target="tpu_custom_call" | custom-call | flops 17179869184 | bytes 16777216 | tf_op jit(solution)/shard_map/pallas_call | solution.py:232
  150.4 0.0 copy-done
  150.4 2.9 %fusion.8 = f32[2,1024,512]{1,2,0:T(8,128)S(1)} fusion(bf16[2,1024,512]{2,1,0:T(8,128)(2,1)} %get-tuple-element.35, bf16[2,1024,512]{2,1,0:T(8,128)(2,1)} %get-tuple-element.5, pred[]{:T(512)S(6)} %eq.16, bf16[512,512]{1,0:T(8,128)(2,1)S(1)} %copy-done), kind=kOutput, calls=%fused_computation.14 | convolution fusion | flops 1074790400 | bytes 8912897 | tf_op jit(solution)/shard_map/dot_general | solution.py:298
  153.3 1.8 fusion.44
  155.0 3.8 %copy.65 = f32[2,1024,4,64]{3,1,2,0:T(8,128)} copy(f32[2,1024,4,64]{1,3,2,0:T(8,128)} %get-tuple-element.13) | data formatting | bytes 4194304
  158.9 0.0 copy-start.8
  158.9 2.7 %copy.66 = f32[2,1024,4,64]{3,1,2,0:T(8,128)} copy(f32[2,1024,4,64]{1,3,2,0:T(8,128)S(1)} %get-tuple-element.12) | data formatting | bytes 4194304
  161.6 0.0 copy-done.8
  161.6 0.1 add_convert_fusion.3
  161.6 0.0 copy-start.5
  161.6 7.1 %multiply_cosine_fusion = (f32[2,1024,64]{2,1,0:T(8,128)}, f32[2,1024,64]{2,1,0:T(8,128)}, f32[2,1024,64]{2,1,0:T(8,128)}, f32[2,1024,64]{2,1,0:T(8,128)}) fusion(f32[2,1024]{1,0:T(2,128)S(1)} %add_convert_fusion.3, f32[64]{0:T(128)S(1)} %multiply_power_fusion, f32[1024]{0:T(1024)S(1)} %iota_convert_fusion), kind=kLoop, calls=%fused_computation.25 | loop fusion | flops 262144 | bytes 2109696 | tf_op jit(solution)/shard_map/cos | solution.py:20
  168.7 0.0 copy-done.5
  168.7 1.3 fusion.10
  170.1 1.8 fusion.45
  171.8 3.8 %copy.63 = f32[2,1024,4,64]{3,1,2,0:T(8,128)} copy(f32[2,1024,4,64]{1,3,2,0:T(8,128)} %get-tuple-element.15) | data formatting | bytes 4194304
  175.6 2.7 %copy.64 = f32[2,1024,4,64]{3,1,2,0:T(8,128)} copy(f32[2,1024,4,64]{1,3,2,0:T(8,128)S(1)} %get-tuple-element.14) | data formatting | bytes 4194304
  178.3 0.0 copy-start.7
  178.3 10.6 %subtract_convert_fusion = (bf16[2,1024,4,64]{3,1,2,0:T(8,128)(2,1)}, bf16[2,1024,4,64]{3,1,2,0:T(8,128)(2,1)}, bf16[2,1024,4,64]{3,1,2,0:T(8,128)(2,1)S(1)}, bf16[2,1024,4,64]{3,1,2,0:T(8,128)(2,1)}) fusion(f32[2,1024,4,64]{3,1,2,0:T(8,128)} %copy.66, f32[2,1024,4,64]{3,1,2,0:T(8,128)} %copy.65, f32[2,1024,64]{2,1,0:T(8,128)} %get-tuple-element.19, ...), kind=kLoop, calls=%fused_computation.1 | loop fusion | flops 8388608 | bytes 14680064 | tf_op jit(solution)/shard_map/convert.1
  189.0 0.1 add_convert_fusion.4
  189.1 0.1 multiply_cosine_fusion.2
  189.2 0.0 copy-done.7
  189.2 0.1 reshape.142
  189.3 0.1 fusion.38
  189.4 0.0 copy-start.2
  189.4 3.8 %fusion.47 = (f32[2,4,4,8]{3,1,2,0:T(4,128)S(1)}, f32[2,4,4,8,1024]{4,3,1,2,0:T(8,128)S(1)}) fusion(bf16[2,1024,4,64]{3,1,2,0:T(8,128)(2,1)} %get-tuple-element.9, bf16[2,1024,4,64]{3,1,2,0:T(8,128)(2,1)} %get-tuple-element.8, bf16[2,4,4,8,64]{4,3,2,1,0:T(8,128)(2,1)S(1)} %get-tuple-element.17, bf16[2,4,4,8,64]{4,3,2,1,0:T(8,128)(2,1)S(1)} %get-tuple-element.16), kind=kOutput, calls=%fused_computation.71 | convolution fusion | flops 71958272 | bytes 3212288 | tf_op jit(solution)/shard_map/cskgd,cmkd->cskgm/dot_general | solution.py:318
  193.1 0.1 iota_compare_fusion.1
  193.2 0.0 copy-done.2
  193.2 0.0 copy-start.6
  193.2 1.4 fusion.46
  194.7 0.0 copy-start.9
  194.7 0.5 fusion.30
  195.1 0.3 copy-done.6
  195.4 0.5 copy-done.9
  195.9 1.3 fusion.19
  197.2 0.0 copy-start.3
  197.2 0.0 copy-start.4
  197.2 0.8 fusion.37
  198.0 0.7 copy-done.3
  198.8 0.6 copy-done.4
  199.4 1.3 fusion.16
  200.7 0.8 fusion.28
  201.6 0.0 copy-start.1
  201.6 0.7 reshape.140
  202.3 1.3 copy.76
  203.6 0.0 copy-done.1
  (6 shorter events, 0.0 us)
Async XLA Ops:
  0.6 149.7 %copy-start = (bf16[512,512]{1,0:T(8,128)(2,1)S(1)}, bf16[512,512]{1,0:T(8,128)(2,1)}, u32[]{:S(2)}) copy-start(bf16[512,512]{1,0:T(8,128)(2,1)} %param.10) | copy-start | bytes 1572868
  158.9 2.7 %copy-start.8 = (s32[2]{0:T(128)S(1)}, s32[2]{0:T(128)}, u32[]{:S(2)}) copy-start(s32[2]{0:T(128)} %param.14) | copy-start | bytes 28
  161.6 7.1 %copy-start.5 = (bf16[2,1024,1024]{2,1,0:T(8,128)(2,1)S(1)}, bf16[2,1024,1024]{2,1,0:T(8,128)(2,1)}, u32[]{:S(2)}) copy-start(bf16[2,1024,1024]{2,1,0:T(8,128)(2,1)} %param.13) | copy-start | bytes 12582916
  178.3 10.9 %copy-start.7 = (bf16[2,4,4096]{2,1,0:T(4,128)(2,1)S(1)}, bf16[2,4,4096]{2,1,0:T(4,128)(2,1)}, u32[]{:S(2)}) copy-start(bf16[2,4,4096]{2,1,0:T(4,128)(2,1)} %param.12) | copy-start | bytes 196612
  189.4 3.8 %copy-start.2 = (bf16[2,1024,4,64]{3,1,2,0:T(8,128)(2,1)S(1)}, bf16[2,1024,4,64]{3,1,2,0:T(8,128)(2,1)}, u32[]{:S(2)}) copy-start(bf16[2,1024,4,64]{3,1,2,0:T(8,128)(2,1)} %get-tuple-element.31) | copy-start | bytes 3145732
  193.2 2.2 %copy-start.6 = (bf16[2,1024,1024]{2,1,0:T(8,128)(2,1)S(1)}, bf16[2,1024,1024]{2,1,0:T(8,128)(2,1)}, u32[]{:S(2)}) copy-start(bf16[2,1024,1024]{2,1,0:T(8,128)(2,1)} %param.13) | copy-start | bytes 12582916
  194.7 1.2 copy-start.9
  197.2 1.6 copy-start.3
  197.2 2.2 %copy-start.4 = (bf16[2,1024,512]{2,1,0:T(8,128)(2,1)S(1)}, bf16[2,1024,512]{2,1,0:T(8,128)(2,1)}, u32[]{:S(2)}) copy-start(bf16[2,1024,512]{2,1,0:T(8,128)(2,1)} %get-tuple-element.5) | copy-start | bytes 6291460
  201.6 2.0 copy-start.1

commit v2 on v1

--- a/solution.py
+++ b/solution.py
@@ -1,7 +1,6 @@
-import functools
-
 import jax
 import jax.numpy as jnp
+import numpy as np
 from jax import lax
 from jax.experimental import pallas as pl
 from jax.experimental.pallas import tpu as pltpu
@@ -35,8 +34,16 @@
     prefill_ref,
     down_ref,
     source_ref,
-    mine_out,
-    other_out,
+    length_ref,
+    query_ref,
+    turn_ref,
+    cosine_ref,
+    sine_ref,
+    up_key_ref,
+    up_value_ref,
+    cache_ref,
+    span_out,
+    attn_ref,
     tokens,
     partial,
     arrived_partial,
@@ -44,8 +51,11 @@
     piece,
     spread,
     staged,
-    mine,
-    other,
+    latents,
+    cached,
+    keys,
+    values,
+    scores,
     load_sem,
     partial_send,
     partial_recv,
@@ -56,6 +66,7 @@
     share_send,
     share_recv,
     store_sem,
+    cache_sem,
 ):
     serve_count, slot_count, rows, width = piece.shape
     tensor = lax.axis_index("tensor")
@@ -112,7 +123,7 @@
         start = pl.multiple_of(place * rows, rows)
         return pltpu.make_async_remote_copy(
             src_ref=staged.at[step],
-            dst_ref=mine.at[:, pl.ds(start, rows), :],
+            dst_ref=latents.at[tensor, :, pl.ds(start, rows), :],
             send_sem=home_send.at[step],
             recv_sem=home_recv.at[place],
             device_id={"serve": target(step)},
@@ -122,14 +133,77 @@
     def share_copy(place):
         start = pl.multiple_of(place * rows, rows)
         return pltpu.make_async_remote_copy(
-            src_ref=mine.at[:, pl.ds(start, rows), :],
-            dst_ref=other.at[:, pl.ds(start, rows), :],
+            src_ref=latents.at[tensor, :, pl.ds(start, rows), :],
+            dst_ref=latents.at[tensor, :, pl.ds(start, rows), :],
             send_sem=share_send.at[place],
             recv_sem=share_recv.at[place],
             device_id={"tensor": peer},
             device_id_type=MESH,
         )
 
+    history = cached.shape[1]
+    kv_count = query_ref.shape[1]
+    score_scale = HEAD_DIM ** (-0.5)
+
+    def write_keys(key_rows, value_rows, cosines, sines, place):
+        key_block = jnp.dot(
+            key_rows.reshape(slot_count * rows, width),
+            up_key_ref[...],
+            preferred_element_type=jnp.float32,
+        )
+        value_block = jnp.dot(
+            value_rows.reshape(slot_count * rows, width),
+            up_value_ref[...],
+            preferred_element_type=jnp.float32,
+        ).astype(jnp.bfloat16)
+        for index in range(slot_count):
+            values[index, pl.ds(place, rows), :] = value_block[index * rows : (index + 1) * rows]
+            for head in range(kv_count):
+                block = key_block[
+                    index * rows : (index + 1) * rows, head * HEAD_DIM : (head + 1) * HEAD_DIM
+                ]
+                turned = pltpu.roll(block, HEAD_DIM // 2, 1)
+                keys[index, pl.ds(place, rows), head * HEAD_DIM : (head + 1) * HEAD_DIM] = (
+                    block * cosines[index] + turned * sines[index]
+                ).astype(jnp.bfloat16)
+
+    def cache_rows(step):
+        place = pl.multiple_of(step * rows, rows)
+        block = cached[:, pl.ds(place, rows), :]
+        cosine = cosine_ref[pl.ds(place, rows), :]
+        sine = sine_ref[pl.ds(place, rows), :]
+        write_keys(
+            block[..., :width], block[..., width:], [cosine] * slot_count, [sine] * slot_count, place
+        )
+
+    def span_rows(place):
+        start = pl.multiple_of(place * rows, rows)
+        cosine = cosine_ref[pl.ds(start, rows), :]
+        sine = sine_ref[pl.ds(start, rows), :]
+        cosines = []
+        sines = []
+        for index in range(slot_count):
+            turn_cosine = turn_ref[0, index : index + 1, :]
+            turn_sine = turn_ref[1, index : index + 1, :]
+            cosines.append(turn_cosine * cosine - turn_sine * sine)
+            sines.append(turn_sine * cosine + turn_cosine * sine)
+        block = latents[:, :, pl.ds(start, rows), :]
+        write_keys(block[0], block[1], cosines, sines, pl.multiple_of(history + start, rows))
+
+    def score(index, head, first, count):
+        block = keys[index, first : first + count, head * HEAD_DIM : (head + 1) * HEAD_DIM]
+        return (
+            lax.dot_general(
+                query_ref[index, head],
+                block,
+                (((1,), (1,)), ((), ())),
+                preferred_element_type=jnp.float32,
+            )
+            * score_scale
+        )
+
+    cache_load = pltpu.make_async_copy(cache_ref, cached, cache_sem.at[0])
+    cache_load.start()
     load(0).start()
     pl.semaphore_wait(barrier, serve_count)
     peer_columns = pl.ds(pl.multiple_of(peer * width, width), width)
@@ -163,9 +237,12 @@
         def _():
             spread[serve] = latent
 
+    cache_load.wait()
+
     @pl.loop(0, serve_count)
     def _(step):
         project(step)
+        cache_rows(step)
 
         @pl.when(step >= LAG)
         def _():
@@ -192,8 +269,21 @@
         @pl.when(step == serve_count - 1)
         def _():
             start = pl.multiple_of(serve * rows, rows)
-            mine[:, pl.ds(start, rows), :] = staged[step]
+            latents[tensor, :, pl.ds(start, rows), :] = staged[step]
             share_copy(serve).start()
+
+    for index in range(slot_count):
+        row = lax.broadcasted_iota(jnp.int32, (query_ref.shape[2], history), 1)
+        live = row < length_ref[index]
+        for head in range(kv_count):
+            scores[index, head, :, :history] = jnp.where(
+                live, score(index, head, 0, history), -jnp.inf
+            )
+
+    def take(step):
+        place = origin(step)
+        share_copy(place).wait_recv()
+        span_rows(place)
 
     @pl.loop(0, serve_count - 1)
     def _(step):
@@ -201,12 +291,46 @@
         home_copy(step, place).wait_recv()
         share_copy(place).start()
 
-    mine_store = pltpu.make_async_copy(mine, mine_out, store_sem.at[0])
-    mine_store.start()
+        @pl.when(step >= LAG)
+        def _():
+            take(step - LAG)
+
+    span_store = pltpu.make_async_copy(latents.at[tensor], span_out, store_sem.at[0])
+    span_store.start()
+
+    @pl.loop(serve_count - 1 - LAG, serve_count)
+    def _(step):
+        take(step)
+
+    span_count = latents.shape[2]
+    for index in range(slot_count):
+        for head in range(kv_count):
+            cache_scores = scores[index, head, :, :history]
+            span_scores = score(index, head, history, span_count)
+            highest = jnp.maximum(
+                jnp.max(cache_scores, axis=-1, keepdims=True),
+                jnp.max(span_scores, axis=-1, keepdims=True),
+            )
+            cache_weights = jnp.exp(cache_scores - highest)
+            span_weights = jnp.exp(span_scores - highest)
+            total = jnp.sum(cache_weights, axis=-1, keepdims=True) + jnp.sum(
+                span_weights, axis=-1, keepdims=True
+            )
+            columns = slice(head * HEAD_DIM, (head + 1) * HEAD_DIM)
+            mixed = jnp.dot(
+                (cache_weights / total).astype(jnp.bfloat16),
+                values[index, :history, columns],
+                preferred_element_type=jnp.float32,
+            ) + jnp.dot(
+                (span_weights / total).astype(jnp.bfloat16),
+                values[index, history:, columns],
+                preferred_element_type=jnp.float32,
+            )
+            attn_ref[index, head] = mixed.astype(jnp.bfloat16)
 
     @pl.loop(0, serve_count)
     def _(step):
-        share_copy(step).wait()
+        share_copy(step).wait_send()
         partial_copy(step).wait_send()
 
         @pl.when(step < serve_count - 1)
@@ -214,13 +338,23 @@
             spread_copy(step, serve).wait_send()
             home_copy(step, serve).wait_send()
 
-    other_store = pltpu.make_async_copy(other, other_out, store_sem.at[1])
-    other_store.start()
-    other_store.wait()
-    mine_store.wait()
-
-
-def hand_off(prefill, down_proj, source_of):
+    span_store.wait()
+
+
+def tables(count):
+    frequency = ROPE_BASE ** (-np.arange(HEAD_DIM // 2) / (HEAD_DIM // 2))
+    angles = np.arange(count)[:, None] * frequency
+    cosine = np.cos(angles)
+    sine = np.sin(angles)
+    return (
+        jnp.asarray(np.concatenate([cosine, cosine], axis=1), jnp.float32),
+        jnp.asarray(np.concatenate([-sine, sine], axis=1), jnp.float32),
+    )
+
+
+def hand_off(
+    prefill, down_proj, source_of, hist_len, rotated, turn, up_key, up_value, cache_latent
+):
     slot_count, span_count, feature_count = prefill.shape
     serve_count = lax.axis_size("serve")
     width = down_proj.shape[1] // lax.axis_size("tensor")
@@ -228,16 +362,17 @@
     half = jax.ShapeDtypeStruct((slot_count, span_count, width), jnp.bfloat16)
     pieces = (serve_count, slot_count, rows, width)
     flat = (serve_count, slot_count * rows, width)
+    history = cache_latent.shape[1]
+    cosine, sine = tables(max(history, span_count))
+    vmem = pl.BlockSpec(memory_space=pltpu.VMEM)
+    smem = pl.BlockSpec(memory_space=pltpu.SMEM)
+    hbm = pl.BlockSpec(memory_space=pl.ANY)
     each = pltpu.SemaphoreType.DMA((serve_count,))
     return pl.pallas_call(
         hand_off_kernel,
-        out_shape=(half, half),
-        in_specs=[
-            pl.BlockSpec(memory_space=pl.ANY),
-            pl.BlockSpec(memory_space=pltpu.VMEM),
-            pl.BlockSpec(memory_space=pltpu.SMEM),
-        ],
-        out_specs=(pl.BlockSpec(memory_space=pl.ANY), pl.BlockSpec(memory_space=pl.ANY)),
+        out_shape=(half, jax.ShapeDtypeStruct(rotated.shape, jnp.bfloat16)),
+        in_specs=[hbm, vmem, smem, smem, vmem, vmem, vmem, vmem, vmem, vmem, hbm],
+        out_specs=(hbm, vmem),
         scratch_shapes=[
             pltpu.VMEM((2, slot_count, rows, feature_count), jnp.bfloat16),
             pltpu.VMEM(flat, jnp.bfloat16),
@@ -246,8 +381,11 @@
             pltpu.VMEM(pieces, jnp.bfloat16),
             pltpu.VMEM(pieces, jnp.bfloat16),
             pltpu.VMEM(pieces, jnp.bfloat16),
-            pltpu.VMEM(half.shape, jnp.bfloat16),
-            pltpu.VMEM(half.shape, jnp.bfloat16),
+            pltpu.VMEM((2,) + half.shape, jnp.bfloat16),
+            pltpu.VMEM(cache_latent.shape, jnp.bfloat16),
+            pltpu.VMEM((slot_count, history + span_count, up_key.shape[1]), jnp.bfloat16),
+            pltpu.VMEM((slot_count, history + span_count, up_key.shape[1]), jnp.bfloat16),
+            pltpu.VMEM(rotated.shape[:3] + (history,), jnp.float32),
             pltpu.SemaphoreType.DMA((2,)),
             each,
             each,
@@ -257,7 +395,8 @@
             each,
             each,
             each,
-            pltpu.SemaphoreType.DMA((2,)),
+            pltpu.SemaphoreType.DMA((1,)),
+            pltpu.SemaphoreType.DMA((1,)),
         ],
         compiler_params=pltpu.CompilerParams(
             collective_id=0, has_side_effects=True, vmem_limit_bytes=56 * 2**20
@@ -267,7 +406,19 @@
             bytes_accessed=2 * slot_count * span_count * feature_count,
             transcendentals=0,
         ),
-    )(prefill, down_proj, source_of)
+    )(
+        prefill,
+        down_proj,
+        source_of,
+        hist_len,
+        rotated,
+        turn,
+        cosine,
+        sine,
+        up_key,
+        up_value,
+        cache_latent,
+    )
 
 
 def shards(prefill, down_proj, up_key, up_value, queries, cache_latent, hist_len, assign):
@@ -275,62 +426,31 @@
     rank_width = down_proj.shape[1] // 2
     request = jnp.arange(assign.shape[0], dtype=jnp.int32)
     source_of = jnp.sum(jnp.where(assign[None, :] == request[:, None], request[None, :], 0), axis=1)
-    span_out, other = hand_off(prefill, down_proj, source_of)
-    first = lax.axis_index("tensor") == 0
-    key_latent = jnp.where(first, span_out, other)
-    value_latent = jnp.where(first, other, span_out)
     kv_local = up_key.shape[1] // HEAD_DIM
     head_local = queries.shape[2] // HEAD_DIM
     group_size = head_local // kv_local
-    history = cache_latent.shape[1]
     step_count = queries.shape[1]
-    score_scale = HEAD_DIM ** (-0.5)
-    cache_keys = jnp.dot(cache_latent[..., :rank_width], up_key, preferred_element_type=jnp.float32)
-    cache_keys = cache_keys.reshape(slot_count, history, kv_local, HEAD_DIM)
-    cache_pos = jnp.broadcast_to(
-        jnp.arange(history, dtype=jnp.int32)[None, :], (slot_count, history)
-    )
-    cache_keys = rotate(cache_keys, cache_pos).astype(jnp.bfloat16)
-    cache_values = jnp.dot(
-        cache_latent[..., rank_width:], up_value, preferred_element_type=jnp.float32
-    ).astype(jnp.bfloat16)
-    cache_values = cache_values.reshape(slot_count, history, kv_local, HEAD_DIM)
-    span_keys = jnp.dot(key_latent, up_key, preferred_element_type=jnp.float32)
-    span_keys = span_keys.reshape(slot_count, span_count, kv_local, HEAD_DIM)
-    span_pos = hist_len[:, None] + jnp.arange(span_count, dtype=jnp.int32)[None, :]
-    span_keys = rotate(span_keys, span_pos).astype(jnp.bfloat16)
-    span_values = jnp.dot(
-        value_latent, up_value, preferred_element_type=jnp.float32
-    ).astype(jnp.bfloat16)
-    span_values = span_values.reshape(slot_count, span_count, kv_local, HEAD_DIM)
     query_pos = hist_len[:, None] + span_count + jnp.arange(step_count, dtype=jnp.int32)[None, :]
     rotated = rotate(
         queries.astype(jnp.float32).reshape(slot_count, step_count, head_local, HEAD_DIM), query_pos
     ).astype(jnp.bfloat16)
-    rotated = rotated.reshape(slot_count, step_count, kv_local, group_size, HEAD_DIM)
-    cache_scores = (
-        jnp.einsum("cskgd,cnkd->cskgn", rotated, cache_keys, preferred_element_type=jnp.float32)
-        * score_scale
-    )
-    live = jnp.arange(history, dtype=jnp.int32)[None, :] < hist_len[:, None]
-    cache_scores = jnp.where(live[:, None, None, None, :], cache_scores, -jnp.inf)
-    span_scores = (
-        jnp.einsum("cskgd,cmkd->cskgm", rotated, span_keys, preferred_element_type=jnp.float32)
-        * score_scale
-    )
-    highest = jnp.maximum(jnp.max(cache_scores, axis=-1), jnp.max(span_scores, axis=-1))
-    cache_weights = jnp.exp(cache_scores - highest[..., None])
-    span_weights = jnp.exp(span_scores - highest[..., None])
-    totals = jnp.sum(cache_weights, axis=-1) + jnp.sum(span_weights, axis=-1)
-    cache_probs = (cache_weights / totals[..., None]).astype(jnp.bfloat16)
-    span_probs = (span_weights / totals[..., None]).astype(jnp.bfloat16)
-    mixed = jnp.einsum(
-        "cskgn,cnkd->cskgd", cache_probs, cache_values, preferred_element_type=jnp.float32
-    )
-    mixed = mixed + jnp.einsum(
-        "cskgm,cmkd->cskgd", span_probs, span_values, preferred_element_type=jnp.float32
-    )
-    attn = mixed.astype(jnp.bfloat16).reshape(slot_count, step_count, head_local * HEAD_DIM)
+    rotated = jnp.swapaxes(
+        rotated.reshape(slot_count, step_count, kv_local, group_size, HEAD_DIM), 1, 2
+    ).reshape(slot_count, kv_local, step_count * group_size, HEAD_DIM)
+    half = HEAD_DIM // 2
+    frequency = ROPE_BASE ** (-jnp.arange(half, dtype=jnp.float32) / half)
+    angles = hist_len.astype(jnp.float32)[:, None] * frequency
+    cosine = jnp.cos(angles)
+    sine = jnp.sin(angles)
+    turn = jnp.stack(
+        [jnp.concatenate([cosine, cosine], axis=1), jnp.concatenate([-sine, sine], axis=1)]
+    )
+    span_out, attn = hand_off(
+        prefill, down_proj, source_of, hist_len, rotated, turn, up_key, up_value, cache_latent
+    )
+    attn = jnp.swapaxes(
+        attn.reshape(slot_count, kv_local, step_count, group_size, HEAD_DIM), 1, 2
+    ).reshape(slot_count, step_count, head_local * HEAD_DIM)
     return (attn, span_out)
 
 

time: 205 us -> 164 us (0.80)
  other arithmetic: 20 us -> 3.88 us
  local copies, waits for them, and re-layouts: 20.8 us -> 5.45 us
  matrix products: 13.7 us -> 0 us
  Pallas kernels: 148 us -> 154 us
    dot_general x8 -> x0, matrix products: 13.7 us -> none  [the longest x1 3.75 us: shards(): jnp.einsum('cskgd,cmkd->cskgm', rotated, span_keys, preferred_element_typ...]
    unnamed x25 -> x1, local copies, waits for them, and re-layouts: 16.5 us -> 3.04 us
    another operation x1 -> x2, other arithmetic: 10.6 us -> 0.67 us  [shards(): jnp.stack([jnp.concatenate([cosine, cosine], axis=1), jnp.concatenate([-s...]
    cos x2 -> x1, other arithmetic: 7.22 us -> 0.12 us  [rotate(): cosine = jnp.cos(angles)]
    pallas_call x1, Pallas kernels: 148 us -> 154 us  [hand_off(): pl.pallas_call(hand_off_kernel, out_shape=(half, jax.ShapeDtypeStruct(rot...]
    slice x2 -> x0, local copies, waits for them, and re-layouts: 3.55 us -> none  [rotate(): second_half = vectors[..., half:]]
where the time goes in v2:
time: 164 us
  Pallas kernels  154 us (94%)
  local copies, waits for them, and re-layouts  5.45 us (3%)
  other arithmetic  3.88 us (2%)
    pallas_call x1, Pallas kernels, hand_off(): pl.pallas_call(hand_off_kernel, out_shape=(half, jax.ShapeDtypeStruct(rot...  154 us

profile of v2, /device:TPU:17, one launch (start us, length us, event | category | flops | bytes accessed | tf_op | source)
XLA Modules:
  0.0 164.1 jit_solution(5603810166968266977)
XLA Ops:
  0.6 1.3 select_reduce_fusion.source_ref
  2.0 0.7 fusion.3
  2.7 0.1 add_convert_fusion.1
  2.8 0.1 multiply_cosine_fusion.1
  2.9 0.1 maximum_bitcast_fusion.1
  3.0 0.6 pad_maximum_fusion.turn_ref
  3.6 0.1 multiply_cosine_fusion
  3.7 0.9 reshape.77
  4.6 0.1 fusion
  4.7 0.7 copy_bitcast_fusion.query_ref
  5.4 154.1 %shard_map.113 = (bf16[2,1024,512]{2,1,0:T(8,128)(2,1)}, bf16[2,4,32,128]{3,2,1,0:T(8,128)(2,1)}) custom-call(bf16[2,1024,4096]{2,1,0:T(8,128)(2,1)} %prefill_ref.1, bf16[4096,1024]{1,0:T(8,128)(2,1)} %down_ref.1, s32[32]{0:T(128)} %select_reduce_fusion.source_ref, s32[2]{0:T(128)} %length_ref.1, bf16[2,4,32,128]{3,2,1,0:T(8,128)(2,1)} %copy_bitcast_fusion.query_ref, ...), custom_call_target="tpu_custom_call" | custom-call | flops 17179869184 | bytes 16777216 | tf_op jit(solution)/shard_map/pallas_call | solution.py:371
  159.5 0.9 copy.16
  160.4 0.7 reshape.75
  161.0 3.0 %copy.19 = bf16[2,1024,512]{2,1,0:T(8,128)(2,1)} copy(bf16[2,1024,512]{2,1,0:T(8,128)(2,1)} %get-tuple-element.20) | data formatting | bytes 4194304
  (1 shorter events, 0.0 us)

commit v3 on v2

--- a/solution.py
+++ b/solution.py
@@ -27,7 +27,8 @@
 
 
 MESH = pl.DeviceIdType.MESH
-LAG = 2
+MATMUL_ROWS = 256
+LEAST_ROWS = 16
 
 
 def hand_off_kernel(
@@ -68,7 +69,12 @@
     store_sem,
     cache_sem,
 ):
-    serve_count, slot_count, rows, width = piece.shape
+    group_count = len(spread)
+    serve_count, slot_count, rows, width = spread[0].shape
+    piece_count = group_count * serve_count
+    batch = tokens.shape[1]
+    batch_count = piece_count // batch
+    group_batches = serve_count // batch
     tensor = lax.axis_index("tensor")
     serve = lax.axis_index("serve")
     peer = 1 - tensor
@@ -91,12 +97,16 @@
     def origin(step):
         return lax.rem(serve + 2 * serve_count - step - 1, serve_count)
 
-    def load(step):
-        start = pl.multiple_of(target(step) * rows, rows)
+    def token_start(group, place):
+        return pl.multiple_of((group * serve_count + place) * rows, rows)
+
+    def load(at, index):
+        step = at * batch + index
+        start = token_start(step // serve_count, target(lax.rem(step, serve_count)))
         return pltpu.make_async_copy(
             prefill_ref.at[:, pl.ds(start, rows), :],
-            tokens.at[lax.rem(step, 2)],
-            load_sem.at[lax.rem(step, 2)],
+            tokens.at[lax.rem(at, 2), index],
+            load_sem.at[lax.rem(at, 2), index],
         )
 
     def partial_copy(step):
@@ -109,34 +119,33 @@
             device_id_type=MESH,
         )
 
-    def spread_copy(step, place):
+    def spread_copy(group, step, place):
         return pltpu.make_async_remote_copy(
-            src_ref=piece.at[step],
-            dst_ref=spread.at[place],
-            send_sem=spread_send.at[step],
-            recv_sem=spread_recv.at[place],
+            src_ref=piece.at[group * serve_count + step],
+            dst_ref=spread[group].at[place],
+            send_sem=spread_send.at[group * serve_count + step],
+            recv_sem=spread_recv.at[group * serve_count + place],
             device_id={"serve": target(step)},
             device_id_type=MESH,
         )
 
-    def home_copy(step, place):
-        start = pl.multiple_of(place * rows, rows)
+    def home_copy(group, step, place):
         return pltpu.make_async_remote_copy(
-            src_ref=staged.at[step],
-            dst_ref=latents.at[tensor, :, pl.ds(start, rows), :],
-            send_sem=home_send.at[step],
-            recv_sem=home_recv.at[place],
+            src_ref=staged.at[group * serve_count + step],
+            dst_ref=latents.at[tensor, :, pl.ds(token_start(group, place), rows), :],
+            send_sem=home_send.at[group * serve_count + step],
+            recv_sem=home_recv.at[group * serve_count + place],
             device_id={"serve": target(step)},
             device_id_type=MESH,
         )
 
-    def share_copy(place):
-        start = pl.multiple_of(place * rows, rows)
+    def share_copy(group, place):
+        part = latents.at[tensor, :, pl.ds(token_start(group, place), rows), :]
         return pltpu.make_async_remote_copy(
-            src_ref=latents.at[tensor, :, pl.ds(start, rows), :],
-            dst_ref=latents.at[tensor, :, pl.ds(start, rows), :],
-            send_sem=share_send.at[place],
-            recv_sem=share_recv.at[place],
+            src_ref=part,
+            dst_ref=part,
+            send_sem=share_send.at[group * serve_count + place],
+            recv_sem=share_recv.at[group * serve_count + place],
             device_id={"tensor": peer},
             device_id_type=MESH,
         )
@@ -145,39 +154,45 @@
     kv_count = query_ref.shape[1]
     score_scale = HEAD_DIM ** (-0.5)
 
-    def write_keys(key_rows, value_rows, cosines, sines, place):
+    def write_keys(key_rows, value_rows, cosines, sines, place, count):
         key_block = jnp.dot(
-            key_rows.reshape(slot_count * rows, width),
+            key_rows.reshape(slot_count * count, width),
             up_key_ref[...],
             preferred_element_type=jnp.float32,
         )
         value_block = jnp.dot(
-            value_rows.reshape(slot_count * rows, width),
+            value_rows.reshape(slot_count * count, width),
             up_value_ref[...],
             preferred_element_type=jnp.float32,
         ).astype(jnp.bfloat16)
         for index in range(slot_count):
-            values[index, pl.ds(place, rows), :] = value_block[index * rows : (index + 1) * rows]
+            values[index, pl.ds(place, count), :] = value_block[index * count : (index + 1) * count]
             for head in range(kv_count):
                 block = key_block[
-                    index * rows : (index + 1) * rows, head * HEAD_DIM : (head + 1) * HEAD_DIM
+                    index * count : (index + 1) * count, head * HEAD_DIM : (head + 1) * HEAD_DIM
                 ]
                 turned = pltpu.roll(block, HEAD_DIM // 2, 1)
-                keys[index, pl.ds(place, rows), head * HEAD_DIM : (head + 1) * HEAD_DIM] = (
+                keys[index, pl.ds(place, count), head * HEAD_DIM : (head + 1) * HEAD_DIM] = (
                     block * cosines[index] + turned * sines[index]
                 ).astype(jnp.bfloat16)
 
+    cache_count = history // batch_count
+
     def cache_rows(step):
-        place = pl.multiple_of(step * rows, rows)
-        block = cached[:, pl.ds(place, rows), :]
-        cosine = cosine_ref[pl.ds(place, rows), :]
-        sine = sine_ref[pl.ds(place, rows), :]
+        place = pl.multiple_of(step * cache_count, cache_count)
+        block = cached[:, pl.ds(place, cache_count), :]
+        cosine = cosine_ref[pl.ds(place, cache_count), :]
+        sine = sine_ref[pl.ds(place, cache_count), :]
         write_keys(
-            block[..., :width], block[..., width:], [cosine] * slot_count, [sine] * slot_count, place
-        )
-
-    def span_rows(place):
-        start = pl.multiple_of(place * rows, rows)
+            block[..., :width],
+            block[..., width:],
+            [cosine] * slot_count,
+            [sine] * slot_count,
+            place,
+            cache_count,
+        )
+
+    def span_rows(start):
         cosine = cosine_ref[pl.ds(start, rows), :]
         sine = sine_ref[pl.ds(start, rows), :]
         cosines = []
@@ -188,7 +203,7 @@
             cosines.append(turn_cosine * cosine - turn_sine * sine)
             sines.append(turn_sine * cosine + turn_cosine * sine)
         block = latents[:, :, pl.ds(start, rows), :]
-        write_keys(block[0], block[1], cosines, sines, pl.multiple_of(history + start, rows))
+        write_keys(block[0], block[1], cosines, sines, pl.multiple_of(history + start, rows), rows)
 
     def score(index, head, first, count):
         block = keys[index, first : first + count, head * HEAD_DIM : (head + 1) * HEAD_DIM]
@@ -204,73 +219,113 @@
 
     cache_load = pltpu.make_async_copy(cache_ref, cached, cache_sem.at[0])
     cache_load.start()
-    load(0).start()
+    for index in range(batch):
+        load(0, index).start()
     pl.semaphore_wait(barrier, serve_count)
     peer_columns = pl.ds(pl.multiple_of(peer * width, width), width)
     own_columns = pl.ds(pl.multiple_of(tensor * width, width), width)
 
-    def project(step):
-        load(step).wait()
-
-        @pl.when(step + 1 < serve_count)
+    def project(at):
+        for index in range(batch):
+            load(at, index).wait()
+
+        @pl.when(at + 1 < batch_count)
         def _():
-            load(step + 1).start()
-
-        block = tokens[lax.rem(step, 2)].reshape(slot_count * rows, -1)
-        partial[step] = jnp.dot(
-            block, down_ref[:, peer_columns], preferred_element_type=jnp.float32
-        ).astype(jnp.bfloat16)
-        partial_copy(step).start()
-        own[step] = jnp.dot(block, down_ref[:, own_columns], preferred_element_type=jnp.float32)
-
-    def finish(step):
-        partial_copy(step).wait_recv()
-        latent = (own[step] + arrived_partial[step].astype(jnp.float32)).astype(jnp.bfloat16)
-        latent = latent.reshape(slot_count, rows, width)
+            for index in range(batch):
+                load(at + 1, index).start()
+
+        block = tokens[lax.rem(at, 2)].reshape(batch * slot_count * rows, -1)
+        steps = pl.ds(pl.multiple_of(at * batch, batch), batch)
+        partial[steps] = (
+            jnp.dot(block, down_ref[:, peer_columns], preferred_element_type=jnp.float32)
+            .astype(jnp.bfloat16)
+            .reshape(batch, slot_count * rows, width)
+        )
+        for index in range(batch):
+            partial_copy(at * batch + index).start()
+        own[steps] = jnp.dot(
+            block, down_ref[:, own_columns], preferred_element_type=jnp.float32
+        ).reshape(batch, slot_count * rows, width)
+
+    def finish(group, step):
+        whole_step = group * serve_count + step
+        partial_copy(whole_step).wait_recv()
+        latent = own[whole_step] + arrived_partial[whole_step].astype(jnp.float32)
+        latent = latent.astype(jnp.bfloat16).reshape(slot_count, rows, width)
 
         @pl.when(step < serve_count - 1)
         def _():
-            piece[step] = latent
-            spread_copy(step, serve).start()
+            piece[whole_step] = latent
+            spread_copy(group, step, serve).start()
 
         @pl.when(step == serve_count - 1)
         def _():
-            spread[serve] = latent
-
-    cache_load.wait()
-
-    @pl.loop(0, serve_count)
-    def _(step):
-        project(step)
-        cache_rows(step)
-
-        @pl.when(step >= LAG)
-        def _():
-            finish(step - LAG)
-
-    @pl.loop(serve_count - LAG, serve_count)
-    def _(step):
-        finish(step)
-
-    @pl.loop(0, serve_count - 1)
-    def _(step):
-        spread_copy(step, origin(step)).wait_recv()
-
-    @pl.loop(0, serve_count)
-    def _(step):
-        for index in range(slot_count):
-            source = source_ref[target(step) * slot_count + index]
-            staged[step, index] = spread[source // slot_count, lax.rem(source, slot_count)]
-
+            spread[group][serve] = latent
+
+    def send_home(group):
+        @pl.loop(0, serve_count - 1)
+        def _(step):
+            spread_copy(group, step, origin(step)).wait_recv()
+
+        @pl.loop(0, serve_count)
+        def _(step):
+            place = group * serve_count + step
+            for index in range(slot_count):
+                source = source_ref[target(step) * slot_count + index]
+                staged[place, index] = spread[group][
+                    source // slot_count, lax.rem(source, slot_count)
+                ]
+
+            @pl.when(step < serve_count - 1)
+            def _():
+                home_copy(group, step, serve).start()
+
+            @pl.when(step == serve_count - 1)
+            def _():
+                latents[tensor, :, pl.ds(token_start(group, serve), rows), :] = staged[place]
+                share_copy(group, serve).start()
+
+    def share(group, step):
         @pl.when(step < serve_count - 1)
         def _():
-            home_copy(step, serve).start()
-
-        @pl.when(step == serve_count - 1)
-        def _():
-            start = pl.multiple_of(serve * rows, rows)
-            latents[tensor, :, pl.ds(start, rows), :] = staged[step]
-            share_copy(serve).start()
+            home_copy(group, step, origin(step)).wait_recv()
+            share_copy(group, origin(step)).start()
+
+    def take(group, step):
+        share_copy(group, origin(step)).wait_recv()
+        span_rows(token_start(group, origin(step)))
+
+    cache_load.wait()
+
+    @pl.loop(0, batch_count)
+    def _(at):
+        project(at)
+        cache_rows(at)
+
+        if group_count > 1:
+
+            @pl.when(at == group_batches + 2)
+            def _():
+                send_home(0)
+
+        for group in range(group_count):
+            first = group * group_batches
+
+            @pl.when((at > first) & (at <= first + group_batches))
+            def _():
+                for index in range(batch):
+                    finish(group, (at - 1 - first) * batch + index)
+
+    for index in range(batch):
+        finish(group_count - 1, serve_count - batch + index)
+
+    if group_count > 1:
+
+        @pl.loop(0, serve_count)
+        def _(step):
+            share(0, step)
+
+    send_home(group_count - 1)
 
     for index in range(slot_count):
         row = lax.broadcasted_iota(jnp.int32, (query_ref.shape[2], history), 1)
@@ -280,27 +335,18 @@
                 live, score(index, head, 0, history), -jnp.inf
             )
 
-    def take(step):
-        place = origin(step)
-        share_copy(place).wait_recv()
-        span_rows(place)
-
-    @pl.loop(0, serve_count - 1)
+    @pl.loop(0, serve_count)
     def _(step):
-        place = origin(step)
-        home_copy(step, place).wait_recv()
-        share_copy(place).start()
-
-        @pl.when(step >= LAG)
-        def _():
-            take(step - LAG)
+        share(group_count - 1, step)
+        if group_count > 1:
+            take(0, step)
 
     span_store = pltpu.make_async_copy(latents.at[tensor], span_out, store_sem.at[0])
     span_store.start()
 
-    @pl.loop(serve_count - 1 - LAG, serve_count)
+    @pl.loop(0, serve_count)
     def _(step):
-        take(step)
+        take(group_count - 1, step)
 
     span_count = latents.shape[2]
     for index in range(slot_count):
@@ -328,15 +374,17 @@
             )
             attn_ref[index, head] = mixed.astype(jnp.bfloat16)
 
-    @pl.loop(0, serve_count)
-    def _(step):
-        share_copy(step).wait_send()
-        partial_copy(step).wait_send()
-
-        @pl.when(step < serve_count - 1)
-        def _():
-            spread_copy(step, serve).wait_send()
-            home_copy(step, serve).wait_send()
+    for group in range(group_count):
+
+        @pl.loop(0, serve_count)
+        def _(step):
+            share_copy(group, step).wait_send()
+            partial_copy(group * serve_count + step).wait_send()
+
+            @pl.when(step < serve_count - 1)
+            def _():
+                spread_copy(group, step, serve).wait_send()
+                home_copy(group, step, serve).wait_send()
 
     span_store.wait()
 
@@ -358,35 +406,38 @@
     slot_count, span_count, feature_count = prefill.shape
     serve_count = lax.axis_size("serve")
     width = down_proj.shape[1] // lax.axis_size("tensor")
-    rows = span_count // serve_count
+    group_count = 2 if span_count % (serve_count * 2 * LEAST_ROWS) == 0 else 1
+    piece_count = group_count * serve_count
+    rows = span_count // piece_count
+    batch = max(1, min(serve_count // 2, MATMUL_ROWS // (slot_count * rows)))
     half = jax.ShapeDtypeStruct((slot_count, span_count, width), jnp.bfloat16)
-    pieces = (serve_count, slot_count, rows, width)
-    flat = (serve_count, slot_count * rows, width)
+    pieces = (piece_count, slot_count, rows, width)
+    flat = (piece_count, slot_count * rows, width)
     history = cache_latent.shape[1]
     cosine, sine = tables(max(history, span_count))
     vmem = pl.BlockSpec(memory_space=pltpu.VMEM)
     smem = pl.BlockSpec(memory_space=pltpu.SMEM)
     hbm = pl.BlockSpec(memory_space=pl.ANY)
-    each = pltpu.SemaphoreType.DMA((serve_count,))
+    each = pltpu.SemaphoreType.DMA((piece_count,))
     return pl.pallas_call(
         hand_off_kernel,
         out_shape=(half, jax.ShapeDtypeStruct(rotated.shape, jnp.bfloat16)),
         in_specs=[hbm, vmem, smem, smem, vmem, vmem, vmem, vmem, vmem, vmem, hbm],
         out_specs=(hbm, vmem),
         scratch_shapes=[
-            pltpu.VMEM((2, slot_count, rows, feature_count), jnp.bfloat16),
+            pltpu.VMEM((2, batch, slot_count, rows, feature_count), jnp.bfloat16),
             pltpu.VMEM(flat, jnp.bfloat16),
             pltpu.VMEM(flat, jnp.bfloat16),
             pltpu.VMEM(flat, jnp.float32),
             pltpu.VMEM(pieces, jnp.bfloat16),
-            pltpu.VMEM(pieces, jnp.bfloat16),
+            [pltpu.VMEM((serve_count,) + pieces[1:], jnp.bfloat16)] * group_count,
             pltpu.VMEM(pieces, jnp.bfloat16),
             pltpu.VMEM((2,) + half.shape, jnp.bfloat16),
             pltpu.VMEM(cache_latent.shape, jnp.bfloat16),
             pltpu.VMEM((slot_count, history + span_count, up_key.shape[1]), jnp.bfloat16),
             pltpu.VMEM((slot_count, history + span_count, up_key.shape[1]), jnp.bfloat16),
             pltpu.VMEM(rotated.shape[:3] + (history,), jnp.float32),
-            pltpu.SemaphoreType.DMA((2,)),
+            pltpu.SemaphoreType.DMA((2, batch)),
             each,
             each,
             each,

time: 164 us -> 145 us (0.88)
  Pallas kernels: 154 us -> 135 us
    pallas_call x1, Pallas kernels: 154 us -> 135 us  [hand_off(): pl.pallas_call(hand_off_kernel, out_shape=(half, jax.ShapeDtypeStruct(rot...]
where the time goes in v3:
time: 145 us
  Pallas kernels  135 us (93%)
  local copies, waits for them, and re-layouts  5.45 us (4%)
  other arithmetic  3.88 us (3%)
    pallas_call x1, Pallas kernels, hand_off(): pl.pallas_call(hand_off_kernel, out_shape=(half, jax.ShapeDtypeStruct(rot...  135 us
    unnamed x1, local copies, waits for them, and re-layouts  3.04 us

profile of v3, /device:TPU:17, one launch (start us, length us, event | category | flops | bytes accessed | tf_op | source)
XLA Modules:
  0.0 145.2 jit_solution(14744152791910042232)
XLA Ops:
  0.6 1.3 select_reduce_fusion.source_ref
  2.0 0.7 fusion.3
  2.7 0.1 add_convert_fusion.1
  2.8 0.1 multiply_cosine_fusion.1
  2.9 0.1 maximum_bitcast_fusion.1
  3.0 0.6 pad_maximum_fusion.turn_ref
  3.6 0.1 multiply_cosine_fusion
  3.7 0.9 reshape.77
  4.6 0.1 fusion
  4.7 0.7 copy_bitcast_fusion.query_ref
  5.4 135.2 %shard_map.113 = (bf16[2,1024,512]{2,1,0:T(8,128)(2,1)}, bf16[2,4,32,128]{3,2,1,0:T(8,128)(2,1)}) custom-call(bf16[2,1024,4096]{2,1,0:T(8,128)(2,1)} %prefill_ref.1, bf16[4096,1024]{1,0:T(8,128)(2,1)} %down_ref.1, s32[32]{0:T(128)} %select_reduce_fusion.source_ref, s32[2]{0:T(128)} %length_ref.1, bf16[2,4,32,128]{3,2,1,0:T(8,128)(2,1)} %copy_bitcast_fusion.query_ref, ...), custom_call_target="tpu_custom_call" | custom-call | flops 17179869184 | bytes 16777216 | tf_op jit(solution)/shard_map/pallas_call | solution.py:422
  140.7 0.9 copy.16
  141.5 0.7 reshape.75
  142.2 3.0 %copy.19 = bf16[2,1024,512]{2,1,0:T(8,128)(2,1)} copy(bf16[2,1024,512]{2,1,0:T(8,128)(2,1)} %get-tuple-element.20) | data formatting | bytes 4194304
  (1 shorter events, 0.0 us)

commit v4 on v3

--- a/solution.py
+++ b/solution.py
@@ -304,7 +304,7 @@
 
         if group_count > 1:
 
-            @pl.when(at == group_batches + 2)
+            @pl.when(at == group_batches + 1)
             def _():
                 send_home(0)
 
@@ -344,6 +344,12 @@
     span_store = pltpu.make_async_copy(latents.at[tensor], span_out, store_sem.at[0])
     span_store.start()
 
+    early = history + (group_count - 1) * serve_count * rows
+    if group_count > 1:
+        for index in range(slot_count):
+            for head in range(kv_count):
+                scores[index, head, :, history:] = score(index, head, history, early - history)
+
     @pl.loop(0, serve_count)
     def _(step):
         take(group_count - 1, step)
@@ -351,8 +357,8 @@
     span_count = latents.shape[2]
     for index in range(slot_count):
         for head in range(kv_count):
-            cache_scores = scores[index, head, :, :history]
-            span_scores = score(index, head, history, span_count)
+            cache_scores = scores[index, head]
+            span_scores = score(index, head, early, history + span_count - early)
             highest = jnp.maximum(
                 jnp.max(cache_scores, axis=-1, keepdims=True),
                 jnp.max(span_scores, axis=-1, keepdims=True),
@@ -365,11 +371,11 @@
             columns = slice(head * HEAD_DIM, (head + 1) * HEAD_DIM)
             mixed = jnp.dot(
                 (cache_weights / total).astype(jnp.bfloat16),
-                values[index, :history, columns],
+                values[index, :early, columns],
                 preferred_element_type=jnp.float32,
             ) + jnp.dot(
                 (span_weights / total).astype(jnp.bfloat16),
-                values[index, history:, columns],
+                values[index, early:, columns],
                 preferred_element_type=jnp.float32,
             )
             attn_ref[index, head] = mixed.astype(jnp.bfloat16)
@@ -436,7 +442,9 @@
             pltpu.VMEM(cache_latent.shape, jnp.bfloat16),
             pltpu.VMEM((slot_count, history + span_count, up_key.shape[1]), jnp.bfloat16),
             pltpu.VMEM((slot_count, history + span_count, up_key.shape[1]), jnp.bfloat16),
-            pltpu.VMEM(rotated.shape[:3] + (history,), jnp.float32),
+            pltpu.VMEM(
+                rotated.shape[:3] + (history + (group_count - 1) * serve_count * rows,), jnp.float32
+            ),
             pltpu.SemaphoreType.DMA((2, batch)),
             each,
             each,

time: 145 us -> 143 us (0.986)
  Pallas kernels: 135 us -> 133 us
    pallas_call x1, Pallas kernels: 135 us -> 133 us  [hand_off(): pl.pallas_call(hand_off_kernel, out_shape=(half, jax.ShapeDtypeStruct(rot...]
where the time goes in v4:
time: 143 us
  Pallas kernels  133 us (93%)
  local copies, waits for them, and re-layouts  5.45 us (4%)
  other arithmetic  3.88 us (3%)
    pallas_call x1, Pallas kernels, hand_off(): pl.pallas_call(hand_off_kernel, out_shape=(half, jax.ShapeDtypeStruct(rot...  133 us
    unnamed x1, local copies, waits for them, and re-layouts  3.04 us

profile of v4, /device:TPU:17, one launch (start us, length us, event | category | flops | bytes accessed | tf_op | source)
XLA Modules:
  0.0 142.6 jit_solution(7320497518082461269)
XLA Ops:
  0.6 1.3 select_reduce_fusion.source_ref
  2.0 0.7 fusion.3
  2.7 0.1 add_convert_fusion.1
  2.8 0.1 multiply_cosine_fusion.1
  2.9 0.1 maximum_bitcast_fusion.1
  3.0 0.6 pad_maximum_fusion.turn_ref
  3.6 0.1 multiply_cosine_fusion
  3.7 0.9 reshape.77
  4.6 0.1 fusion
  4.7 0.7 copy_bitcast_fusion.query_ref
  5.4 132.6 %shard_map.113 = (bf16[2,1024,512]{2,1,0:T(8,128)(2,1)}, bf16[2,4,32,128]{3,2,1,0:T(8,128)(2,1)}) custom-call(bf16[2,1024,4096]{2,1,0:T(8,128)(2,1)} %prefill_ref.1, bf16[4096,1024]{1,0:T(8,128)(2,1)} %down_ref.1, s32[32]{0:T(128)} %select_reduce_fusion.source_ref, s32[2]{0:T(128)} %length_ref.1, bf16[2,4,32,128]{3,2,1,0:T(8,128)(2,1)} %copy_bitcast_fusion.query_ref, ...), custom_call_target="tpu_custom_call" | custom-call | flops 17179869184 | bytes 16777216 | tf_op jit(solution)/shard_map/pallas_call | solution.py:428
  138.0 0.9 copy.16
  138.9 0.7 reshape.75
  139.5 3.0 %copy.19 = bf16[2,1024,512]{2,1,0:T(8,128)(2,1)} copy(bf16[2,1024,512]{2,1,0:T(8,128)(2,1)} %get-tuple-element.20) | data formatting | bytes 4194304
  (1 shorter events, 0.0 us)
